TPU v7x, 768 devices: a whole 4x8x12 slice. The times are simulated.
768 devices in a mesh: fsdp: 48 (over z, x_hi, core), rep: 16 (over x_lo, y).
Axes of the slice: x: 4 (x_hi: 2, x_lo: 2; x = x_hi * 2 + x_lo), y: 8, z: 12, core: 2. Of those that a mesh axis runs over, the one named last changes fastest.
Arguments:
- local_params: float32 [16, 18432, 1024], P('rep', 'fsdp'), may hold values from -400 to 400
- global_params: float32 [18432, 1024], P('fsdp'), may hold values from -6 to 6
- momentum: float32 [18432, 1024], P(('fsdp', 'rep')), may hold values from -4 to 4
Outputs:
- new_global: float32 [18432, 1024], P('fsdp')
- new_momentum: float32 [18432, 1024], P(('fsdp', 'rep'))
- mixed: float32 [16, 18432, 1024], P('rep', 'fsdp')
All inputs are finite; a program needn't handle non-finite values.
Results may differ from a plain program's by a relative error of at most 0.005.
Values may be sent and summed in bfloat16 or wider, within the bound.
A program may use at most 32 MiB of HBM per device.

v0:
```python
import jax
import jax.numpy as jnp
from jax import lax
from jax.sharding import PartitionSpec as P

GROUP = 128


EPS = 1e-06
CLIP = 0.3
MU = 0.9
RATE = 0.7
MIXING = 0.5


def shards(local_params, global_params, momentum):
    local = local_params[0]
    rows, cols = local.shape
    groups_row = cols // GROUP
    replicas = lax.axis_size("rep")
    share = rows // replicas
    delta = global_params - local
    grouped = delta.reshape(rows, groups_row, GROUP)
    scale = ((jnp.max(jnp.abs(grouped), axis=2) + EPS) / 127.0).astype(jnp.bfloat16)
    wide_scale = scale.astype(jnp.float32)[:, :, None]
    coded = (grouped / wide_scale).astype(jnp.bfloat16)
    term = (coded.astype(jnp.float32) * wide_scale).reshape(rows, cols)
    summed = lax.psum_scatter(term, "rep", scatter_dimension=0, tiled=True)
    pseudo = summed / replicas
    total_sq = lax.psum(jnp.sum(pseudo * pseudo), ("fsdp", "rep"))
    count = rows * cols * lax.axis_size("fsdp")
    rms = jnp.sqrt(total_sq / count)
    factor = CLIP / jnp.maximum(rms, CLIP)
    clipped = pseudo * factor
    new_momentum = MU * momentum + clipped
    offset = lax.axis_index("rep") * share
    owned = lax.dynamic_slice_in_dim(global_params, offset, share, 0)
    updated = owned - RATE * (clipped + MU * new_momentum)
    new_global = lax.all_gather(updated, "rep", axis=0, tiled=True)
    mixed = MIXING * new_global[None] + (1.0 - MIXING) * local_params
    return (new_global, new_momentum, mixed)


def solution(mesh):
    placed = (P("rep", "fsdp", None), P("fsdp", None), P(("fsdp", "rep"), None))
    return jax.shard_map(
        shards,
        mesh=mesh,
        in_specs=placed,
        out_specs=(P("fsdp", None), P(("fsdp", "rep"), None), P("rep", "fsdp", None)),
        check_vma=False,
    )
```

profile of v0, /device:TPU:4, one launch (start us, length us, event | category | flops | bytes accessed | tf_op | source)
XLA Modules:
  0.0 289.5 jit_solution(14376072647576887415)
XLA Ops:
  7.2 0.0 reduce-scatter.2.cloned.1.call-start
  7.2 2.3 abs_bitcast_fusion
  9.5 1.5 copy.9
  11.0 0.0 copy-start
  11.0 0.0 copy-start.1
  11.0 2.0 reduce_max.9
  13.0 0.1 copy.7
  13.1 0.2 copy.8
  13.3 0.5 div.31
  13.8 0.0 copy-done
  13.8 0.0 copy-done.1
  13.8 1.9 bitcast_multiply_fusion
  15.6 0.0 copy-start.3
  15.6 0.0 reduce-scatter.2.cloned.1.call-update
  15.6 0.0 all-gather.2.cloned.1.call-start
  15.7 84.3 %reduce-scatter.2.cloned.1.call-done = f32[24,1024]{1,0:T(8,128)} async-done(((f32[384,1024]{1,0:T(8,128)}), f32[24,1024]{1,0:T(8,128)}) %reduce-scatter.2.cloned.1.call-update) | async-done | bytes 98320 | tf_op jit(solution)/shard_map/reduce_scatter | solution.py:28
  100.0 1.5 multiply_reduce_fusion
  101.5 107.2 %psum.7 = f32[]{:T(128)} all-reduce(f32[]{:T(128)} %multiply_reduce_fusion), channel_id=1, replica_groups=mesh['fsdp'=48,'rep'=16] {'fsdp','rep'}, use_global_device_ids=true, to_apply=%region_3.0 | all-reduce | flops 1 | bytes 8 | tf_op jit(solution)/shard_map/psum | solution.py:30
  209.5 0.0 copy-done.3
  209.5 1.6 multiply_subtract_fusion
  211.1 0.0 all-gather.2.cloned.1.call-update
  211.1 67.3 %all-gather.2.cloned.1.call-done = f32[384,1024]{1,0:T(8,128)} async-done(((f32[24,1024]{1,0:T(8,128)}), f32[384,1024]{1,0:T(8,128)}) %all-gather.2.cloned.1.call-update) | async-done | bytes 1572880 | tf_op jit(solution)/shard_map/all_gather | solution.py:39
  278.4 0.0 copy-start.2
  278.4 3.1 %fusion.1 = f32[1,384,1024]{2,1,0:T(8,128)} fusion(f32[1,384,1024]{2,1,0:T(8,128)S(1)} %copy-done, f32[384,1024]{1,0:T(8,128)} %all-gather.2.cloned.1.call-done), kind=kLoop, calls=%fused_computation.4 | loop fusion | flops 786432 | bytes 4718592 | tf_op jit(solution)/shard_map/add | solution.py:40
  281.5 0.0 copy-done.2
  281.5 1.1 copy.16
  (1 shorter events, 0.0 us)
Async XLA Ops:
  7.2 92.8 %reduce-scatter.2.cloned.1.call-start = ((), (), s32[]{:S(2)}) async-start(), calls=%async_computation.1 | async-start | bytes 1671168 | tf_op jit(solution)/shard_map/reduce_scatter | solution.py:28
  11.0 2.8 copy-start
  11.0 2.8 copy-start.1
  15.6 193.8 %copy-start.3 = (f32[24,1024]{1,0:T(8,128)S(1)}, f32[24,1024]{1,0:T(8,128)}, u32[]{:S(2)}) copy-start(f32[24,1024]{1,0:T(8,128)} %param.5) | copy-start | bytes 294916
  15.6 262.7 %all-gather.2.cloned.1.call-start = ((), (), s32[]{:S(2)}) async-start(), calls=%async_computation.2 | async-start | bytes 1671168 | tf_op jit(solution)/shard_map/all_gather | solution.py:39
  278.4 3.1 %copy-start.2 = (f32[384,1024]{1,0:T(8,128)S(1)}, f32[384,1024]{1,0:T(8,128)}, u32[]{:S(2)}) copy-start(f32[384,1024]{1,0:T(8,128)} %all-gather.2.cloned.1.call-done) | copy-start | bytes 4718596
Sparse Core Ops, SparseCore 0:
  15.8 84.1 reduce-scatter.1
  211.2 67.1 all-gather.1
where the time goes:
time: 290 us; the launch traced here: 289 us
  waiting for transfers between devices  152 us (52%)
  blocking collectives  107 us (37%)
  between operations  14.8 us (5%)
  other arithmetic  12.4 us (4%)
  local copies, waits for them, and re-layouts  3.33 us (1%)
    psum x1, blocking collectives, shards(): total_sq = lax.psum(jnp.sum(pseudo * pseudo), ('fsdp', 'rep'))  107 us
    reduce_scatter x1, waiting for transfers between devices, shards(): summed = lax.psum_scatter(term, 'rep', scatter_dimension=0, tiled=True)  84.3 us
    all_gather x1, waiting for transfers between devices, shards(): new_global = lax.all_gather(updated, 'rep', axis=0, tiled=True)  67.3 us
  transfers between devices with their start and end apart: 2, of which 2 were waited for; matrix products, arithmetic and copies ran while one was open for 0% of the time, Pallas kernels for 0%

commit v1 on v0

v1 whole, which is shorter than its diff:
```python
import functools

import jax
import jax.numpy as jnp
from jax import lax
from jax.experimental import pallas as pl
from jax.experimental.pallas import tpu as pltpu
from jax.sharding import PartitionSpec as P

EPS = 1e-06
CLIP = 0.3
MU = 0.9
RATE = 0.7
MIXING = 0.5

MESH = pl.DeviceIdType.MESH
NY = 8
NXL = 2
NXH = 2
NZ = 12
REPS = NXL * NY
COLS = 1024
HALF = COLS // 2
SHARE = 24
BLK = 2 * SHARE
ROWS = SHARE * REPS
COUNT = float(ROWS * COLS * NZ * NXH * 2)
ORDER = (4, 3, 5, 2, 6, 1, 7, 0)


def fold(v):
    return jnp.concatenate([v[:, :HALF], v[:, HALF:]], axis=0)


def unfold(v):
    return jnp.concatenate([v[:SHARE], v[SHARE:]], axis=1)


def exchange(
    local_hbm, global_hbm, mom_hbm,
    pg, mg, pown, fout,
    lv, gv, mv, xs, xr, ys, yr, src, ary, arx, arz,
    load, rxs, rxr, rys, ryr, pys, pyr, pxs, pxr, mys, myr, mxs, mxr,
    ays, ayr, axs, axr, azs, azr,
):
    f = lax.axis_index("fsdp")
    r = lax.axis_index("rep")
    core = f % 2
    xh = (f // 2) % NXH
    z = f // (2 * NXH)
    a = r // NY
    y = r % NY
    other = 1 - a
    half_rows = ROWS // NXL

    def in_y(k):
        return a * NY + (y + k) % NY

    def y_dev(k):
        return (f, in_y(k))

    x_dev = (f, other * NY + y)

    loads = []
    for i, col in enumerate((other, a)):
        rows = pl.ds(pl.multiple_of(col * half_rows, 8), half_rows)
        for j, (s, d) in enumerate(((local_hbm, lv), (global_hbm, gv))):
            cp = pltpu.make_async_copy(s.at[rows], d.at[rows], load.at[2 * i + j])
            cp.start()
            loads.append(cp)
    mcp = pltpu.make_async_copy(mom_hbm, mv, load.at[4])
    mcp.start()

    ar_y = [y_dev(k) for k in range(1, NY)]
    ar_x = []
    for i in range(4):
        for j in range(2):
            if i or j:
                xx = (xh * 2 + a + i) % 4
                ar_x.append(((z * NXH + xx // 2) * 2 + (core + j) % 2, (xx % 2) * NY + y))
    ar_z = [((((z + k) % NZ) * NXH + xh) * 2 + core, r) for k in range(1, NZ)]
    barrier = pltpu.get_barrier_semaphore()
    partners = ar_y + ar_x + ar_z
    for d in partners:
        pl.semaphore_signal(barrier, inc=1, device_id=d, device_id_type=MESH)

    def remote(s, d, ss, rs, dev):
        return pltpu.make_async_remote_copy(
            src_ref=s, dst_ref=d, send_sem=ss, recv_sem=rs, device_id=dev, device_id_type=MESH
        )

    def delta(d):
        rows = pl.ds(pl.multiple_of(d * SHARE, 8), SHARE)
        return fold(gv[rows, :] - lv[rows, :])

    loads[0].wait()
    loads[1].wait()
    for k in ORDER:
        xs[k] = delta(other * NY + (y + k) % NY).astype(jnp.bfloat16)
    mcp.wait()
    mg[r] = fold(mv[...]).astype(jnp.bfloat16)

    pl.semaphore_wait(barrier, len(partners))

    sends = []

    def go(s, d, ss, rs, dev):
        cp = remote(s, d, ss, rs, dev)
        cp.start()
        sends.append(cp)
        return cp

    rx = {}
    for k in ORDER:
        rx[k] = go(xs.at[k], xr.at[k], rxs.at[k], rxr.at[k], x_dev)
    my = {}
    for k in (1, 7, 2, 6):
        my[k] = go(mg.at[r], mg.at[r], mys.at[k], myr.at[k], y_dev(k))
    loads[2].wait()
    loads[3].wait()
    ry = {}
    for k in ORDER:
        rx[k].wait_recv()
        v = delta(in_y(k)) + xr[k].astype(jnp.float32)
        if k:
            ys[k] = v.astype(jnp.bfloat16)
            ry[k] = go(ys.at[k], yr.at[k], rys.at[k], ryr.at[k], y_dev(k))
        else:
            total = v
    def got(arr, k):
        return arr.at[in_y(-k)]

    my[2].wait_recv()
    my[6].wait_recv()
    my[3] = go(got(mg, 2), got(mg, 2), mys.at[3], myr.at[3], y_dev(1))
    my[5] = go(got(mg, 6), got(mg, 6), mys.at[5], myr.at[5], y_dev(7))
    my[4] = go(got(mg, 2), got(mg, 2), mys.at[4], myr.at[4], y_dev(2))
    mx = {}
    mx[0] = go(mg.at[r], mg.at[r], mxs.at[0], mxr.at[0], x_dev)
    my[1].wait_recv()
    my[7].wait_recv()
    for k in (1, 7, 2, 6):
        mx[k] = go(got(mg, k), got(mg, k), mxs.at[k], mxr.at[k], x_dev)
    for k in (4, 3, 5, 2, 6, 1, 7):
        ry[k].wait_recv()
        total = total + yr[k].astype(jnp.float32)
    p = total * (1.0 / REPS)
    pown[...] = p
    sq = p * p
    sq = jnp.sum(sq, axis=0, keepdims=True)
    sq = sq[:, 0:128] + sq[:, 128:256] + sq[:, 256:384] + sq[:, 384:512]
    src[0] = sq
    ar = []
    for j, d in enumerate(ar_y):
        ar.append(go(src.at[0], ary.at[j], ays.at[j], ayr.at[j], d))
    pg[r] = p.astype(jnp.bfloat16)
    py = {}
    px = {}
    px[0] = go(pg.at[r], pg.at[r], pxs.at[0], pxr.at[0], x_dev)
    for k in (1, 7, 2, 6, 3, 5, 4):
        py[k] = go(pg.at[r], pg.at[r], pys.at[k], pyr.at[k], y_dev(k))

    def forward(ks):
        for k in ks:
            py[k].wait_recv()
            px[k] = go(got(pg, k), got(pg, k), pxs.at[k], pxr.at[k], x_dev)

    for cp in ar:
        cp.wait_recv()
    sq = sq + jnp.sum(ary[...], axis=0)
    src[1] = sq
    ar = []
    for j, d in enumerate(ar_x):
        ar.append(go(src.at[1], arx.at[j], axs.at[j], axr.at[j], d))
    forward((1, 7))
    for cp in ar:
        cp.wait_recv()
    sq = sq + jnp.sum(arx[...], axis=0)
    src[2] = sq
    ar = []
    for j, d in enumerate(ar_z):
        ar.append(go(src.at[2], arz.at[j], azs.at[j], azr.at[j], d))
    for k in (3, 5, 4):
        my[k].wait_recv()
        mx[k] = go(got(mg, k), got(mg, k), mxs.at[k], mxr.at[k], x_dev)
    forward((2, 6, 3, 5, 4))
    for cp in ar:
        cp.wait_recv()
    sq = sq + jnp.sum(arz[...], axis=0)
    rms = jnp.sqrt(jnp.sum(sq, axis=1, keepdims=True) * (1.0 / COUNT))
    fout[...] = jnp.broadcast_to(CLIP / jnp.maximum(rms, CLIP), fout.shape)
    for k in range(NY):
        mx[k].wait_recv()
        px[k].wait_recv()
    for cp in sends:
        cp.wait_send()


def finish(f_ref, pown, mom, pg, mg, local, glob, new_global, new_momentum, mixed):
    factor = f_ref[0:1, 0:1]
    g = glob.shape[0] // SHARE

    @pl.when(pl.program_id(0) == 0)
    def _():
        new_momentum[...] = MU * mom[...] + factor * unfold(pown[...])

    cp = factor * (RATE * (1.0 + MU))
    for i in range(g):
        rows = pl.ds(i * SHARE, SHARE)
        step = cp * pg[i].astype(jnp.float32) + (RATE * MU * MU) * mg[i].astype(jnp.float32)
        updated = glob[rows, :] - unfold(step)
        new_global[rows, :] = updated
        mixed[rows, :] = MIXING * updated + (1.0 - MIXING) * local[rows, :]


def shards(local_params, global_params, momentum):
    local = local_params[0]
    bf, f32 = jnp.bfloat16, jnp.float32
    vmem = pl.BlockSpec(memory_space=pltpu.VMEM)
    hbm = pl.BlockSpec(memory_space=pl.ANY)
    dma = pltpu.SemaphoreType.DMA
    gathered = jax.ShapeDtypeStruct((REPS, BLK, HALF), bf)
    pg, mg, pown, factor = pl.pallas_call(
        exchange,
        name="exchange",
        out_shape=[
            gathered,
            gathered,
            jax.ShapeDtypeStruct((BLK, HALF), f32),
            jax.ShapeDtypeStruct((8, 128), f32),
        ],
        in_specs=[hbm] * 3,
        out_specs=[vmem] * 4,
        scratch_shapes=[
            pltpu.VMEM((ROWS, COLS), f32),
            pltpu.VMEM((ROWS, COLS), f32),
            pltpu.VMEM((SHARE, COLS), f32),
            pltpu.VMEM((NY, BLK, HALF), bf),
            pltpu.VMEM((NY, BLK, HALF), bf),
            pltpu.VMEM((NY, BLK, HALF), bf),
            pltpu.VMEM((NY, BLK, HALF), bf),
            pltpu.VMEM((3, 1, 128), f32),
            pltpu.VMEM((NY - 1, 1, 128), f32),
            pltpu.VMEM((7, 1, 128), f32),
            pltpu.VMEM((NZ - 1, 1, 128), f32),
            dma((5,)),
        ]
        + [dma((NY,))] * 12
        + [dma((NY - 1,))] * 2
        + [dma((7,))] * 2
        + [dma((NZ - 1,))] * 2,
        compiler_params=pltpu.CompilerParams(
            collective_id=0, has_side_effects=True, vmem_limit_bytes=20 << 20
        ),
    )(local, global_params, momentum)

    steps = 4
    rows = ROWS // steps
    wide = pl.BlockSpec((rows, COLS), lambda i: (i, 0))
    blocks = pl.BlockSpec((REPS // steps, BLK, HALF), lambda i: (i, 0, 0))
    whole = lambda *s: pl.BlockSpec(s, lambda i: (0,) * len(s))
    new_global, new_momentum, mixed = pl.pallas_call(
        finish,
        name="finish",
        grid=(steps,),
        out_shape=[
            jax.ShapeDtypeStruct((ROWS, COLS), f32),
            jax.ShapeDtypeStruct((SHARE, COLS), f32),
            jax.ShapeDtypeStruct((ROWS, COLS), f32),
        ],
        in_specs=[whole(8, 128), whole(BLK, HALF), whole(SHARE, COLS), blocks, blocks, wide, wide],
        out_specs=[wide, whole(SHARE, COLS), wide],
        compiler_params=pltpu.CompilerParams(vmem_limit_bytes=16 << 20),
    )(factor, pown, momentum, pg, mg, local, global_params)
    return (new_global, new_momentum, mixed[None])


def solution(mesh):
    placed = (P("rep", "fsdp", None), P("fsdp", None), P(("fsdp", "rep"), None))
    return jax.shard_map(
        shards,
        mesh=mesh,
        in_specs=placed,
        out_specs=(P("fsdp", None), P(("fsdp", "rep"), None), P("rep", "fsdp", None)),
        check_vma=False,
    )
```

time: 290 us -> 60.9 us (0.21)
  the two profiles are of different devices: /device:TPU:4 before, /device:TPU:1 now
where the time goes in v1:
time: 60.9 us; the launch traced here: 60.7 us
  Pallas kernels  56.3 us (92%)
  local copies, waits for them, and re-layouts  3.7 us (6%)
  between operations  0.66 us (1%)
    pallas_call x1, Pallas kernels, shards(): pl.pallas_call(exchange, name='exchange', out_shape=[gathered, gathered,...  53.9 us
    unnamed x8, local copies, waits for them, and re-layouts  3.7 us
    pallas_call x1, Pallas kernels, shards(): pl.pallas_call(finish, name='finish', grid=(steps,), out_shape=[jax.Shape...  2.4 us

profile of v1, /device:TPU:1, one launch (start us, length us, event | category | flops | bytes accessed | tf_op | source)
XLA Modules:
  0.0 60.7 jit_solution(11488322179943517708)
XLA Ops:
  0.6 0.0 copy-start
  0.6 1.4 %copy-done = f32[1,384,1024]{2,1,0:T(8,128)S(1)} copy-done((f32[1,384,1024]{2,1,0:T(8,128)S(1)}, f32[1,384,1024]{2,1,0:T(8,128)}, u32[]{:S(2)}) %copy-start) | copy-done | bytes 1572888
  2.0 0.0 copy-start.2
  2.0 1.4 %copy-done.2 = f32[384,1024]{1,0:T(8,128)S(1)} copy-done((f32[384,1024]{1,0:T(8,128)S(1)}, f32[384,1024]{1,0:T(8,128)}, u32[]{:S(2)}) %copy-start.2) | copy-done | bytes 1572888
  3.4 0.0 copy-start.3
  3.5 0.9 %copy-done.3 = f32[24,1024]{1,0:T(8,128)S(1)} copy-done((f32[24,1024]{1,0:T(8,128)S(1)}, f32[24,1024]{1,0:T(8,128)}, u32[]{:S(2)}) %copy-start.3) | copy-done | bytes 98328
  4.3 0.0 copy-start.1
  4.3 53.9 %exchange.1 = (bf16[16,48,512]{2,1,0:T(8,128)(2,1)S(1)}, bf16[16,48,512]{2,1,0:T(8,128)(2,1)S(1)}, f32[48,512]{1,0:T(8,128)S(1)}, f32[8,128]{1,0:T(8,128)S(1)}) custom-call(f32[384,1024]{1,0:T(8,128)S(1)} %bitcast.2, f32[384,1024]{1,0:T(8,128)S(1)} %copy-done.2, f32[24,1024]{1,0:T(8,128)S(1)} %copy-done.3), custom_call_target="tpu_custom_call" | custom-call | tf_op jit(solution)/shard_map/exchange/pallas_call | solution.py:223
  58.3 0.0 copy-done.1
  58.3 2.4 %finish.1 = (f32[384,1024]{1,0:T(8,128)}, f32[24,1024]{1,0:T(8,128)}, f32[384,1024]{1,0:T(8,128)}) custom-call(f32[8,128]{1,0:T(8,128)S(1)} %get-tuple-element.10.f_ref, f32[48,512]{1,0:T(8,128)S(1)} %get-tuple-element.11.pown, f32[24,1024]{1,0:T(8,128)S(1)} %copy-done.3, bf16[16,48,512]{2,1,0:T(8,128)(2,1)S(1)} %get-tuple-element.12.pg, ...), custom_call_target="tpu_custom_call" | custom-call | tf_op jit(solution)/shard_map/finish/pallas_call | solution.py:262
Async XLA Ops:
  0.6 1.4 %copy-start = (f32[1,384,1024]{2,1,0:T(8,128)S(1)}, f32[1,384,1024]{2,1,0:T(8,128)}, u32[]{:S(2)}) copy-start(f32[1,384,1024]{2,1,0:T(8,128)} %param.3) | copy-start | bytes 4718596
  2.0 1.4 %copy-start.2 = (f32[384,1024]{1,0:T(8,128)S(1)}, f32[384,1024]{1,0:T(8,128)}, u32[]{:S(2)}) copy-start(f32[384,1024]{1,0:T(8,128)} %glob.1) | copy-start | bytes 4718596
  3.4 0.9 %copy-start.3 = (f32[24,1024]{1,0:T(8,128)S(1)}, f32[24,1024]{1,0:T(8,128)}, u32[]{:S(2)}) copy-start(f32[24,1024]{1,0:T(8,128)} %mom.1) | copy-start | bytes 294916
  4.3 53.9 %copy-start.1 = (f32[1,384,1024]{2,1,0:T(8,128)S(1)}, f32[1,384,1024]{2,1,0:T(8,128)}, u32[]{:S(2)}) copy-start(f32[1,384,1024]{2,1,0:T(8,128)} %param.3) | copy-start | bytes 4718596

commit v2 on v1

v2 whole, which is shorter than its diff:
```python
import functools

import jax
import jax.numpy as jnp
from jax import lax
from jax.experimental import pallas as pl
from jax.experimental.pallas import tpu as pltpu
from jax.sharding import PartitionSpec as P

EPS = 1e-06
CLIP = 0.3
MU = 0.9
RATE = 0.7
MIXING = 0.5

MESH = pl.DeviceIdType.MESH
NY = 8
NXL = 2
NXH = 2
NX = NXL * NXH
NZ = 12
REPS = NXL * NY
COLS = 1024
HALF = COLS // 2
SHARE = 24
BLK = 2 * SHARE
ROWS = SHARE * REPS
COUNT = float(ROWS * COLS * NZ * NXH * 2)
N_XY = NX * NY - 1
N_ZC = 2 * NZ - 1
ORDER = (4, 3, 5, 2, 6, 1, 7, 0)


def fold(v):
    return jnp.concatenate([v[:, :HALF], v[:, HALF:]], axis=0)


def exchange(
    local_hbm, global_hbm, mom_hbm,
    pg, mg, pown, fout,
    lv, gv, mv, xs, xr, ys, yr, src, arxy, arzc,
    load, ssem, rxr, ryr, pyr, pxr, pnr, myr, mxr, asr, up,
):
    bf, f32 = jnp.bfloat16, jnp.float32
    f = lax.axis_index("fsdp")
    r = lax.axis_index("rep")
    core = f % 2
    xh = (f // 2) % NXH
    z = f // (2 * NXH)
    a = r // NY
    y = r % NY

    def wrap(t, n):
        return jnp.where(t >= n, t - n, t)

    yy = [y] + [wrap(y + k, NY) for k in range(1, NY)]
    col, ocol = a * NY, NY - a * NY
    own = [col + v for v in yy]
    oth = [ocol + v for v in yy]
    x_dev = (f, oth[0])

    def y_dev(k):
        return (f, own[k])

    loads = []
    half_rows = ROWS // NXL
    for i, c in enumerate((ocol, col)):
        rows = pl.ds(pl.multiple_of(c * SHARE, 8), half_rows)
        for j, (s, d) in enumerate(((local_hbm, lv), (global_hbm, gv))):
            cp = pltpu.make_async_copy(s.at[rows], d.at[rows], load.at[2 * i + j])
            cp.start()
            loads.append(cp)
    mcp = pltpu.make_async_copy(mom_hbm, mv, load.at[4])
    mcp.start()

    def far(steps, n):
        return min(steps, n - steps)

    xx = [xh * NXL + a] + [wrap(xh * NXL + a + i, NX) for i in range(1, NX)]
    fx = [z * (2 * NXH) + core + (v // NXL) * 2 for v in xx]
    rx0 = [(v % NXL) * NY for v in xx]
    near = sorted(((far(i, NX) + far(k, NY), i, k) for i in range(NX) for k in range(NY) if i or k), reverse=True)
    ar_xy = [(fx[i], rx0[i] + yy[k]) for _, i, k in near]
    def plane(zt, c):
        return ((zt * NXH + xh) * 2 + c, r)

    def to_planes(test, what):
        for zt in range(NZ):
            pl.when(test(zt))(functools.partial(what, zt))

    barrier = pltpu.get_barrier_semaphore()
    for d in ar_xy + [plane(z, 1 - core)]:
        pl.semaphore_signal(barrier, inc=1, device_id=d, device_id_type=MESH)

    def announce(sem, zt):
        for c in range(2):
            pl.semaphore_signal(sem, inc=1, device_id=plane(zt, c), device_id_type=MESH)

    to_planes(lambda zt: zt > z, functools.partial(announce, barrier))

    def remote(s, d, ss, rs, dev):
        return pltpu.make_async_remote_copy(
            src_ref=s, dst_ref=d, send_sem=ss, recv_sem=rs, device_id=dev, device_id_type=MESH
        )

    sent = {}

    def go(s, d, flow, rs, dev):
        cp = remote(s, d, ssem.at[flow], rs, dev)
        cp.start()
        sent[flow] = sent.get(flow, 0) + 1
        return cp

    def drain(flow):
        q = pg.at[pl.ds(0, sent[flow])]
        remote(q, q, ssem.at[flow], ssem.at[flow], x_dev).wait_send()

    seen = set()

    def arrived(cp):
        if id(cp) not in seen:
            seen.add(id(cp))
            cp.wait_recv()

    def delta(d):
        rows = pl.ds(pl.multiple_of(d * SHARE, 8), SHARE)
        return fold(gv[rows, :] - lv[rows, :])

    loads[0].wait()
    loads[1].wait()
    for k in ORDER:
        xs[k] = delta(oth[k]).astype(bf)
    pl.semaphore_wait(barrier, N_XY + 1 + 2 * z)

    def slot(buf, k):
        return buf.at[own[(NY - k) % NY]]

    def first(buf, flow, sems):
        return {k: go(buf.at[r], buf.at[r], flow, sems.at[k], y_dev(k)) for k in (2, 6, 1, 7)}

    def second(buf, flow, sems, got):
        arrived(got[2])
        got[3] = go(slot(buf, 2), slot(buf, 2), flow, sems.at[3], y_dev(1))
        arrived(got[6])
        got[5] = go(slot(buf, 6), slot(buf, 6), flow, sems.at[5], y_dev(7))
        s = buf.at[jnp.where(core == 0, own[6], own[2])]
        got[4] = go(s, s, flow, sems.at[4], (f, jnp.where(core == 0, own[2], own[6])))

    def over(buf, flow, sems, got, ks):
        res = {}
        for k in ks:
            if k:
                arrived(got[k])
            res[k] = go(slot(buf, k), slot(buf, k), flow, sems.at[k], x_dev)
        return res

    rx = {k: go(xs.at[k], xr.at[k], 0, rxr.at[k], x_dev) for k in ORDER}
    mcp.wait()
    mg[r] = fold(mv[...]).astype(bf)
    my = first(mg, 4, myr)
    to_planes(lambda zt: zt < z, functools.partial(announce, up))
    loads[2].wait()
    loads[3].wait()
    ry = {}
    for k in ORDER:
        rx[k].wait_recv()
        v = delta(own[k]) + xr[k].astype(f32)
        if k:
            ys[k] = v.astype(bf)
            ry[k] = go(ys.at[k], yr.at[k], 1, ryr.at[k], y_dev(k))
        else:
            total = v
    mx = over(mg, 5, mxr, my, (0, 1, 7, 2, 6))
    for k in ORDER[:-1]:
        ry[k].wait_recv()
        total = total + yr[k].astype(f32)
    p = total * (1.0 / REPS)
    sq = jnp.sum(p * p, axis=0, keepdims=True)
    sq = sq[:, 0:128] + sq[:, 128:256] + sq[:, 256:384] + sq[:, 384:512]
    src[0] = sq
    for j, d in enumerate(ar_xy):
        remote(src.at[0], arxy.at[j], asr.at[0], asr.at[1], d).start()

    pown[...] = p
    pg[r] = p.astype(bf)

    px = over(pg, 3, pxr, None, (0,))
    py = first(pg, 2, pyr)
    second(mg, 4, myr, my)

    pltpu.make_async_copy(arxy, arxy, asr.at[1]).wait()
    sq = sq + jnp.sum(arxy[...], axis=0)
    src[1] = sq
    mine = 2 * z + core
    arzc[mine] = sq

    def share(zt, c):
        remote(src.at[1], arzc.at[mine], asr.at[2], asr.at[3], plane(zt, c)).start()

    def share_both(zt):
        for c in range(2):
            share(zt, c)

    to_planes(lambda zt: zt < z, share_both)
    share(z, 1 - core)

    @pl.when(z < NZ - 1)
    def _():
        pl.semaphore_wait(up, 2 * (NZ - 1 - z))

    to_planes(lambda zt: zt > z, share_both)

    arrived(px[0])
    q = pg.at[oth[0]]
    pn = [go(q, q, 2, pnr.at[i], y_dev(k)) for i, k in enumerate((1, 7))]
    second(pg, 2, pyr, py)
    px.update(over(pg, 3, pxr, py, (2, 6)))
    mx.update(over(mg, 5, mxr, my, (3, 5, 4)))
    px.update(over(pg, 3, pxr, py, (3, 5, 4)))
    for cp in [py[1], py[7]] + pn + list(px.values()) + list(mx.values()):
        arrived(cp)
    for flow in range(6):
        drain(flow)
    remote(arxy, arxy, asr.at[0], asr.at[0], x_dev).wait_send()
    others = arzc.at[pl.ds(0, N_ZC)]
    remote(others, others, asr.at[2], asr.at[2], x_dev).wait_send()

    pltpu.make_async_copy(others, others, asr.at[3]).wait()
    sq = jnp.sum(arzc[...], axis=0)
    rms = jnp.sqrt(jnp.sum(sq, axis=1, keepdims=True) * (1.0 / COUNT))
    fout[...] = jnp.broadcast_to(CLIP / jnp.maximum(rms, CLIP), fout.shape)


def finish(f_ref, pown, mom, pg, mg, local, glob, new_global, new_momentum, mixed):
    factor = f_ref[0:1, 0:1]
    halves = [(0, pl.ds(0, HALF)), (SHARE, pl.ds(HALF, HALF))]

    @pl.when(pl.program_id(0) == 0)
    def _():
        for top, cols in halves:
            new_momentum[:, cols] = MU * mom[:, cols] + factor * pown[top:top + SHARE]

    cp = factor * (RATE * (1.0 + MU))
    for b in range(glob.shape[0] // SHARE):
        rows = pl.ds(b * SHARE, SHARE)
        step = cp * pg[b].astype(jnp.float32) + (RATE * MU * MU) * mg[b].astype(jnp.float32)
        for top, cols in halves:
            updated = glob[rows, cols] - step[top:top + SHARE]
            new_global[rows, cols] = updated
            mixed[rows, cols] = MIXING * updated + (1.0 - MIXING) * local[rows, cols]


def shards(local_params, global_params, momentum):
    local = local_params[0]
    bf, f32 = jnp.bfloat16, jnp.float32
    vmem = pl.BlockSpec(memory_space=pltpu.VMEM)
    hbm = pl.BlockSpec(memory_space=pltpu.HBM)
    dma = pltpu.SemaphoreType.DMA
    gathered = jax.ShapeDtypeStruct((REPS, BLK, HALF), bf)
    in_hbm = [pltpu.with_memory_space_constraint(v, pltpu.HBM) for v in (local, global_params, momentum)]
    pg, mg, pown, factor = pl.pallas_call(
        exchange,
        name="exchange",
        out_shape=[
            gathered,
            gathered,
            jax.ShapeDtypeStruct((BLK, HALF), f32),
            jax.ShapeDtypeStruct((8, 128), f32),
        ],
        in_specs=[hbm] * 3,
        out_specs=[vmem] * 4,
        scratch_shapes=[
            pltpu.VMEM((ROWS, COLS), f32),
            pltpu.VMEM((ROWS, COLS), f32),
            pltpu.VMEM((SHARE, COLS), f32),
        ]
        + [pltpu.VMEM((NY, BLK, HALF), bf)] * 4
        + [
            pltpu.VMEM((2, 1, 128), f32),
            pltpu.VMEM((N_XY, 1, 128), f32),
            pltpu.VMEM((N_ZC + 1, 1, 128), f32),
            dma((5,)),
            dma((6,)),
            dma((NY,)),
            dma((NY,)),
            dma((NY,)),
            dma((NY,)),
            dma((2,)),
            dma((NY,)),
            dma((NY,)),
            dma((4,)),
            pltpu.SemaphoreType.REGULAR,
        ],
        compiler_params=pltpu.CompilerParams(
            collective_id=0, has_side_effects=True, vmem_limit_bytes=20 << 20
        ),
    )(*in_hbm)

    steps = 4
    wide = pl.BlockSpec((ROWS // steps, COLS), lambda i: (i, 0))
    blocks = pl.BlockSpec((REPS // steps, BLK, HALF), lambda i: (i, 0, 0))

    def whole(*s):
        return pl.BlockSpec(s, lambda i: (0,) * len(s))

    new_global, new_momentum, mixed = pl.pallas_call(
        finish,
        name="finish",
        grid=(steps,),
        out_shape=[
            jax.ShapeDtypeStruct((ROWS, COLS), f32),
            jax.ShapeDtypeStruct((SHARE, COLS), f32),
            jax.ShapeDtypeStruct((ROWS, COLS), f32),
        ],
        in_specs=[whole(8, 128), whole(BLK, HALF), whole(SHARE, COLS), blocks, blocks, wide, wide],
        out_specs=[wide, whole(SHARE, COLS), wide],
        compiler_params=pltpu.CompilerParams(vmem_limit_bytes=16 << 20),
    )(factor, pown, momentum, pg, mg, local, global_params)
    return (new_global, new_momentum, mixed[None])


def solution(mesh):
    placed = (P("rep", "fsdp", None), P("fsdp", None), P(("fsdp", "rep"), None))
    return jax.shard_map(
        shards,
        mesh=mesh,
        in_specs=placed,
        out_specs=(P("fsdp", None), P(("fsdp", "rep"), None), P("rep", "fsdp", None)),
        check_vma=False,
    )
```

time: 60.9 us -> 47.7 us (0.78)
  Pallas kernels: 56.3 us -> 46.9 us
  local copies, waits for them, and re-layouts: 3.7 us -> 0.01 us
    pallas_call x1, Pallas kernels: 53.9 us -> 44.4 us  [shards(): pl.pallas_call(exchange, name='exchange', out_shape=[gathered, gathered,...]
    unnamed x8 -> x6, local copies, waits for them, and re-layouts: 3.7 us -> 0.01 us
where the time goes in v2:
time: 47.7 us; the launch traced here: 47.5 us
  Pallas kernels  46.9 us (98%)
  between operations  0.69 us (1%)
    pallas_call x1, Pallas kernels, shards(): pl.pallas_call(exchange, name='exchange', out_shape=[gathered, gathered,...  44.4 us
    pallas_call x1, Pallas kernels, shards(): pl.pallas_call(finish, name='finish', grid=(steps,), out_shape=[jax.Shape...  2.4 us

profile of v2, /device:TPU:1, one launch (start us, length us, event | category | flops | bytes accessed | tf_op | source)
XLA Modules:
  0.0 47.5 jit_solution(9494660385593300336)
XLA Ops:
  0.6 0.0 copy-start
  0.6 0.0 copy-start.1
  0.7 0.0 copy-start.2
  0.7 44.4 %exchange.1 = (bf16[16,48,512]{2,1,0:T(8,128)(2,1)S(1)}, bf16[16,48,512]{2,1,0:T(8,128)(2,1)S(1)}, f32[48,512]{1,0:T(8,128)S(1)}, f32[8,128]{1,0:T(8,128)S(1)}) custom-call(f32[384,1024]{1,0:T(8,128)} %bitcast.2, f32[384,1024]{1,0:T(8,128)} %glob.1, f32[24,1024]{1,0:T(8,128)} %mom.1), custom_call_target="tpu_custom_call" | custom-call | tf_op jit(solution)/shard_map/exchange/pallas_call | solution.py:261
  45.1 0.0 copy-done
  45.1 0.0 copy-done.1
  45.1 0.0 copy-done.2
  45.1 2.4 %finish.1 = (f32[384,1024]{1,0:T(8,128)}, f32[24,1024]{1,0:T(8,128)}, f32[384,1024]{1,0:T(8,128)}) custom-call(f32[8,128]{1,0:T(8,128)S(1)} %get-tuple-element.10.f_ref, f32[48,512]{1,0:T(8,128)S(1)} %get-tuple-element.11.pown, f32[24,1024]{1,0:T(8,128)S(1)} %copy-done.2, bf16[16,48,512]{2,1,0:T(8,128)(2,1)S(1)} %get-tuple-element.12.pg, ...), custom_call_target="tpu_custom_call" | custom-call | tf_op jit(solution)/shard_map/finish/pallas_call | solution.py:306
Async XLA Ops:
  0.6 44.5 %copy-start = (f32[1,384,1024]{2,1,0:T(8,128)S(1)}, f32[1,384,1024]{2,1,0:T(8,128)}, u32[]{:S(2)}) copy-start(f32[1,384,1024]{2,1,0:T(8,128)} %param.3) | copy-start | bytes 4718596
  0.6 44.5 %copy-start.1 = (f32[384,1024]{1,0:T(8,128)S(1)}, f32[384,1024]{1,0:T(8,128)}, u32[]{:S(2)}) copy-start(f32[384,1024]{1,0:T(8,128)} %glob.1) | copy-start | bytes 4718596
  0.7 44.5 %copy-start.2 = (f32[24,1024]{1,0:T(8,128)S(1)}, f32[24,1024]{1,0:T(8,128)}, u32[]{:S(2)}) copy-start(f32[24,1024]{1,0:T(8,128)} %mom.1) | copy-start | bytes 294916

commit v3 on v2

--- a/solution.py
+++ b/solution.py
@@ -28,7 +28,9 @@
 COUNT = float(ROWS * COLS * NZ * NXH * 2)
 N_XY = NX * NY - 1
 N_ZC = 2 * NZ - 1
-ORDER = (4, 3, 5, 2, 6, 1, 7, 0)
+STEPS = 4
+ORDER = (3, 5, 2, 6, 1, 7)
+FAR = NY // 2
 
 
 def fold(v):
@@ -38,8 +40,8 @@
 def exchange(
     local_hbm, global_hbm, mom_hbm,
     pg, mg, pown, fout,
-    lv, gv, mv, xs, xr, ys, yr, src, arxy, arzc,
-    load, ssem, rxr, ryr, pyr, pxr, pnr, myr, mxr, asr, up,
+    lv, gv, mv, xs, xr, ys, yr, fs, fr, src, arxy, arzc,
+    load, ssem, rxr, ryr, far_sem, pyr, pxr, pnr, myr, mxr, asr, up, hop, pair, side, both,
 ):
     bf, f32 = jnp.bfloat16, jnp.float32
     f = lax.axis_index("fsdp")
@@ -88,15 +90,31 @@
         for zt in range(NZ):
             pl.when(test(zt))(functools.partial(what, zt))
 
-    barrier = pltpu.get_barrier_semaphore()
-    for d in ar_xy + [plane(z, 1 - core)]:
-        pl.semaphore_signal(barrier, inc=1, device_id=d, device_id_type=MESH)
+    def tell(sem, d):
+        pl.semaphore_signal(sem, inc=1, device_id=d, device_id_type=MESH)
 
     def announce(sem, zt):
         for c in range(2):
-            pl.semaphore_signal(sem, inc=1, device_id=plane(zt, c), device_id_type=MESH)
+            tell(sem, plane(zt, c))
+
+    beside = ((z * NXH + 1 - xh) * 2 + core, r)
+    barrier = pltpu.get_barrier_semaphore()
+    for d in (y_dev(FAR), x_dev, y_dev(1), y_dev(NY - 1), plane(z, 1 - core)):
+        tell(barrier, d)
+
+    @pl.when(xh == 0)
+    def _():
+        tell(barrier, beside)
 
     to_planes(lambda zt: zt > z, functools.partial(announce, barrier))
+
+    def hop_out(level):
+        tell(hop.at[level, 0], y_dev(1))
+        tell(hop.at[level, 1], y_dev(NY - 1))
+
+    def hop_in(level):
+        pl.semaphore_wait(hop.at[level, 0], 1)
+        pl.semaphore_wait(hop.at[level, 1], 1)
 
     def remote(s, d, ss, rs, dev):
         return pltpu.make_async_remote_copy(
@@ -128,9 +146,10 @@
 
     loads[0].wait()
     loads[1].wait()
+    fs[0] = delta(oth[FAR]).astype(bf)
     for k in ORDER:
         xs[k] = delta(oth[k]).astype(bf)
-    pl.semaphore_wait(barrier, N_XY + 1 + 2 * z)
+    pl.semaphore_wait(barrier, 5 + xh + 2 * z)
 
     def slot(buf, k):
         return buf.at[own[(NY - k) % NY]]
@@ -154,30 +173,56 @@
             res[k] = go(slot(buf, k), slot(buf, k), flow, sems.at[k], x_dev)
         return res
 
+    def send_far(i):
+        return go(fs.at[i], fr.at[i], 6, far_sem.at[i], y_dev(FAR))
+
+    hop_out(0)
+    rf = [send_far(0)]
     rx = {k: go(xs.at[k], xr.at[k], 0, rxr.at[k], x_dev) for k in ORDER}
+    loads[2].wait()
+    loads[3].wait()
+    fs[1] = delta(own[FAR]).astype(bf)
+    rf.append(send_far(1))
+    hop_in(0)
+    hop_out(1)
+
+    @pl.when(xh == 1)
+    def _():
+        tell(side, beside)
+
     mcp.wait()
     mg[r] = fold(mv[...]).astype(bf)
-    my = first(mg, 4, myr)
+    hop_in(1)
+    tell(pair, x_dev)
     to_planes(lambda zt: zt < z, functools.partial(announce, up))
-    loads[2].wait()
-    loads[3].wait()
     ry = {}
     for k in ORDER:
         rx[k].wait_recv()
-        v = delta(own[k]) + xr[k].astype(f32)
-        if k:
-            ys[k] = v.astype(bf)
-            ry[k] = go(ys.at[k], yr.at[k], 1, ryr.at[k], y_dev(k))
-        else:
-            total = v
-    mx = over(mg, 5, mxr, my, (0, 1, 7, 2, 6))
-    for k in ORDER[:-1]:
+        ys[k] = (delta(own[k]) + xr[k].astype(f32)).astype(bf)
+        ry[k] = go(ys.at[k], yr.at[k], 1, ryr.at[k], y_dev(k))
+        if k == ORDER[2]:
+            pl.semaphore_wait(pair, 1)
+
+            @pl.when(xh == 0)
+            def _():
+                pl.semaphore_wait(side, 1)
+
+            tell(both, beside)
+    rf[0].wait_recv()
+    xs[0] = (delta(oth[0]) + fr[0].astype(f32)).astype(bf)
+    rx[0] = go(xs.at[0], xr.at[0], 0, rxr.at[0], x_dev)
+    rf[1].wait_recv()
+    total = delta(own[0]) + fr[1].astype(f32)
+    for k in ORDER:
         ry[k].wait_recv()
         total = total + yr[k].astype(f32)
+    rx[0].wait_recv()
+    total = total + xr[0].astype(f32)
     p = total * (1.0 / REPS)
     sq = jnp.sum(p * p, axis=0, keepdims=True)
     sq = sq[:, 0:128] + sq[:, 128:256] + sq[:, 256:384] + sq[:, 384:512]
     src[0] = sq
+    pl.semaphore_wait(both, 1)
     for j, d in enumerate(ar_xy):
         remote(src.at[0], arxy.at[j], asr.at[0], asr.at[1], d).start()
 
@@ -186,7 +231,8 @@
 
     px = over(pg, 3, pxr, None, (0,))
     py = first(pg, 2, pyr)
-    second(mg, 4, myr, my)
+    my = first(mg, 4, myr)
+    mx = over(mg, 5, mxr, my, (0,))
 
     pltpu.make_async_copy(arxy, arxy, asr.at[1]).wait()
     sq = sq + jnp.sum(arxy[...], axis=0)
@@ -215,11 +261,13 @@
     pn = [go(q, q, 2, pnr.at[i], y_dev(k)) for i, k in enumerate((1, 7))]
     second(pg, 2, pyr, py)
     px.update(over(pg, 3, pxr, py, (2, 6)))
+    second(mg, 4, myr, my)
+    mx.update(over(mg, 5, mxr, my, (2, 6, 1, 7)))
+    px.update(over(pg, 3, pxr, py, (3, 5, 4)))
     mx.update(over(mg, 5, mxr, my, (3, 5, 4)))
-    px.update(over(pg, 3, pxr, py, (3, 5, 4)))
     for cp in [py[1], py[7]] + pn + list(px.values()) + list(mx.values()):
         arrived(cp)
-    for flow in range(6):
+    for flow in range(7):
         drain(flow)
     remote(arxy, arxy, asr.at[0], asr.at[0], x_dev).wait_send()
     others = arzc.at[pl.ds(0, N_ZC)]
@@ -231,23 +279,32 @@
     fout[...] = jnp.broadcast_to(CLIP / jnp.maximum(rms, CLIP), fout.shape)
 
 
-def finish(f_ref, pown, mom, pg, mg, local, glob, new_global, new_momentum, mixed):
+def finish(f_ref, pown, mom, pg, mg, local, glob, new_global, new_momentum, mixed, gbuf, mbuf, xbuf, sem):
     factor = f_ref[0:1, 0:1]
     halves = [(0, pl.ds(0, HALF)), (SHARE, pl.ds(HALF, HALF))]
-
-    @pl.when(pl.program_id(0) == 0)
-    def _():
-        for top, cols in halves:
-            new_momentum[:, cols] = MU * mom[:, cols] + factor * pown[top:top + SHARE]
-
     cp = factor * (RATE * (1.0 + MU))
-    for b in range(glob.shape[0] // SHARE):
-        rows = pl.ds(b * SHARE, SHARE)
-        step = cp * pg[b].astype(jnp.float32) + (RATE * MU * MU) * mg[b].astype(jnp.float32)
-        for top, cols in halves:
-            updated = glob[rows, cols] - step[top:top + SHARE]
-            new_global[rows, cols] = updated
-            mixed[rows, cols] = MIXING * updated + (1.0 - MIXING) * local[rows, cols]
+    copies = []
+    per = REPS // STEPS
+    for t in range(STEPS):
+        for b in range(t * per, (t + 1) * per):
+            rows = pl.ds(b * SHARE, SHARE)
+            step = cp * pg[b].astype(jnp.float32) + (RATE * MU * MU) * mg[b].astype(jnp.float32)
+            for top, cols in halves:
+                updated = glob[rows, cols] - step[top:top + SHARE]
+                gbuf[rows, cols] = updated
+                xbuf[rows, cols] = MIXING * updated + (1.0 - MIXING) * local[rows, cols]
+        rows = pl.ds(t * per * SHARE, per * SHARE)
+        for i, (s, d) in enumerate(((gbuf, new_global), (xbuf, mixed))):
+            q = pltpu.make_async_copy(s.at[rows], d.at[rows], sem.at[2 * t + i])
+            q.start()
+            copies.append(q)
+    for top, cols in halves:
+        mbuf[:, cols] = MU * mom[:, cols] + factor * pown[top:top + SHARE]
+    q = pltpu.make_async_copy(mbuf, new_momentum, sem.at[2 * STEPS])
+    q.start()
+    copies.append(q)
+    for q in copies:
+        q.wait()
 
 
 def shards(local_params, global_params, momentum):
@@ -275,20 +332,26 @@
             pltpu.VMEM((SHARE, COLS), f32),
         ]
         + [pltpu.VMEM((NY, BLK, HALF), bf)] * 4
+        + [pltpu.VMEM((2, BLK, HALF), bf)] * 2
         + [
             pltpu.VMEM((2, 1, 128), f32),
             pltpu.VMEM((N_XY, 1, 128), f32),
             pltpu.VMEM((N_ZC + 1, 1, 128), f32),
             dma((5,)),
-            dma((6,)),
-            dma((NY,)),
-            dma((NY,)),
+            dma((7,)),
             dma((NY,)),
             dma((NY,)),
             dma((2,)),
             dma((NY,)),
             dma((NY,)),
+            dma((2,)),
+            dma((NY,)),
+            dma((NY,)),
             dma((4,)),
+            pltpu.SemaphoreType.REGULAR,
+            pltpu.SemaphoreType.REGULAR((2, 2)),
+            pltpu.SemaphoreType.REGULAR,
+            pltpu.SemaphoreType.REGULAR,
             pltpu.SemaphoreType.REGULAR,
         ],
         compiler_params=pltpu.CompilerParams(
@@ -296,24 +359,23 @@
         ),
     )(*in_hbm)
 
-    steps = 4
-    wide = pl.BlockSpec((ROWS // steps, COLS), lambda i: (i, 0))
-    blocks = pl.BlockSpec((REPS // steps, BLK, HALF), lambda i: (i, 0, 0))
-
-    def whole(*s):
-        return pl.BlockSpec(s, lambda i: (0,) * len(s))
-
+    any_space = pl.BlockSpec(memory_space=pl.ANY)
     new_global, new_momentum, mixed = pl.pallas_call(
         finish,
         name="finish",
-        grid=(steps,),
         out_shape=[
             jax.ShapeDtypeStruct((ROWS, COLS), f32),
             jax.ShapeDtypeStruct((SHARE, COLS), f32),
             jax.ShapeDtypeStruct((ROWS, COLS), f32),
         ],
-        in_specs=[whole(8, 128), whole(BLK, HALF), whole(SHARE, COLS), blocks, blocks, wide, wide],
-        out_specs=[wide, whole(SHARE, COLS), wide],
+        in_specs=[vmem] * 7,
+        out_specs=[any_space] * 3,
+        scratch_shapes=[
+            pltpu.VMEM((ROWS, COLS), f32),
+            pltpu.VMEM((SHARE, COLS), f32),
+            pltpu.VMEM((ROWS, COLS), f32),
+            dma((2 * STEPS + 1,)),
+        ],
         compiler_params=pltpu.CompilerParams(vmem_limit_bytes=16 << 20),
     )(factor, pown, momentum, pg, mg, local, global_params)
     return (new_global, new_momentum, mixed[None])

time: 47.7 us -> 46.2 us (0.969)
  Pallas kernels: 46.9 us -> 45.3 us
    pallas_call x1, Pallas kernels: 44.4 us -> 43.4 us  [shards(): pl.pallas_call(exchange, name='exchange', out_shape=[gathered, gathered,...]
    pallas_call x1, Pallas kernels: 2.4 us -> 1.9 us  [shards(): pl.pallas_call(finish, name='finish', out_shape=[jax.ShapeDtypeStruct((RO...]
where the time goes in v3:
time: 46.2 us; the launch traced here: 46 us
  Pallas kernels  45.3 us (98%)
  between operations  0.69 us (1%)
    pallas_call x1, Pallas kernels, shards(): pl.pallas_call(exchange, name='exchange', out_shape=[gathered, gathered,...  43.4 us
    pallas_call x1, Pallas kernels, shards(): pl.pallas_call(finish, name='finish', out_shape=[jax.ShapeDtypeStruct((RO...  1.9 us

profile of v3, /device:TPU:1, one launch (start us, length us, event | category | flops | bytes accessed | tf_op | source)
XLA Modules:
  0.0 46.0 jit_solution(17850501149511081520)
XLA Ops:
  0.6 0.0 copy-start
  0.6 0.0 copy-start.1
  0.7 0.0 copy-start.2
  0.7 43.4 %exchange.1 = (bf16[16,48,512]{2,1,0:T(8,128)(2,1)S(1)}, bf16[16,48,512]{2,1,0:T(8,128)(2,1)S(1)}, f32[48,512]{1,0:T(8,128)S(1)}, f32[8,128]{1,0:T(8,128)S(1)}) custom-call(f32[384,1024]{1,0:T(8,128)} %bitcast.2, f32[384,1024]{1,0:T(8,128)} %glob.1, f32[24,1024]{1,0:T(8,128)} %mom.1), custom_call_target="tpu_custom_call" | custom-call | tf_op jit(solution)/shard_map/exchange/pallas_call | solution.py:318
  44.1 0.0 copy-done
  44.1 0.0 copy-done.1
  44.1 0.0 copy-done.2
  44.1 1.9 %finish.1 = (f32[384,1024]{1,0:T(8,128)}, f32[24,1024]{1,0:T(8,128)}, f32[384,1024]{1,0:T(8,128)}) custom-call(f32[8,128]{1,0:T(8,128)S(1)} %get-tuple-element.10.f_ref, f32[48,512]{1,0:T(8,128)S(1)} %get-tuple-element.11.pown, f32[24,1024]{1,0:T(8,128)S(1)} %copy-done.2, bf16[16,48,512]{2,1,0:T(8,128)(2,1)S(1)} %get-tuple-element.12.pg, ...), custom_call_target="tpu_custom_call" | custom-call | tf_op jit(solution)/shard_map/finish/pallas_call | solution.py:363
Async XLA Ops:
  0.6 43.5 %copy-start = (f32[1,384,1024]{2,1,0:T(8,128)S(1)}, f32[1,384,1024]{2,1,0:T(8,128)}, u32[]{:S(2)}) copy-start(f32[1,384,1024]{2,1,0:T(8,128)} %param.3) | copy-start | bytes 4718596
  0.6 43.5 %copy-start.1 = (f32[384,1024]{1,0:T(8,128)S(1)}, f32[384,1024]{1,0:T(8,128)}, u32[]{:S(2)}) copy-start(f32[384,1024]{1,0:T(8,128)} %glob.1) | copy-start | bytes 4718596
  0.7 43.5 %copy-start.2 = (f32[24,1024]{1,0:T(8,128)S(1)}, f32[24,1024]{1,0:T(8,128)}, u32[]{:S(2)}) copy-start(f32[24,1024]{1,0:T(8,128)} %mom.1) | copy-start | bytes 294916

commit v4 on v3

--- a/solution.py
+++ b/solution.py
@@ -25,6 +25,7 @@
 SHARE = 24
 BLK = 2 * SHARE
 ROWS = SHARE * REPS
+FIRST = 4
 COUNT = float(ROWS * COLS * NZ * NXH * 2)
 N_XY = NX * NY - 1
 N_ZC = 2 * NZ - 1
@@ -39,9 +40,9 @@
 
 def exchange(
     local_hbm, global_hbm, mom_hbm,
-    pg, mg, pown, fout,
-    lv, gv, mv, xs, xr, ys, yr, fs, fr, src, arxy, arzc,
-    load, ssem, rxr, ryr, far_sem, pyr, pxr, pnr, myr, mxr, asr, up, hop, pair, side, both,
+    pg, mg, pown, fout, lv, gv, mv,
+    xs, xr, ys, yr, fs, fr, src, arxy, arzc,
+    load, ssem, rxr, ryr, far_sem, pyr, pxr, pnr, myr, mxr, mnr, asr, up, hop, pair, side, both,
 ):
     bf, f32 = jnp.bfloat16, jnp.float32
     f = lax.axis_index("fsdp")
@@ -165,6 +166,10 @@
         s = buf.at[jnp.where(core == 0, own[6], own[2])]
         got[4] = go(s, s, flow, sems.at[4], (f, jnp.where(core == 0, own[2], own[6])))
 
+    def pass_on(buf, flow, sems):
+        q = buf.at[oth[0]]
+        return [go(q, q, flow, sems.at[i], y_dev(k)) for i, k in enumerate((1, 7))]
+
     def over(buf, flow, sems, got, ks):
         res = {}
         for k in ks:
@@ -192,11 +197,16 @@
 
     mcp.wait()
     mg[r] = fold(mv[...]).astype(bf)
+    mx = over(mg, 5, mxr, None, (0,))
     hop_in(1)
     tell(pair, x_dev)
     to_planes(lambda zt: zt < z, functools.partial(announce, up))
     ry = {}
     for k in ORDER:
+        if k == ORDER[-1]:
+            rf[0].wait_recv()
+            xs[0] = (delta(oth[0]) + fr[0].astype(f32)).astype(bf)
+            rx[0] = go(xs.at[0], xr.at[0], 0, rxr.at[0], x_dev)
         rx[k].wait_recv()
         ys[k] = (delta(own[k]) + xr[k].astype(f32)).astype(bf)
         ry[k] = go(ys.at[k], yr.at[k], 1, ryr.at[k], y_dev(k))
@@ -208,9 +218,6 @@
                 pl.semaphore_wait(side, 1)
 
             tell(both, beside)
-    rf[0].wait_recv()
-    xs[0] = (delta(oth[0]) + fr[0].astype(f32)).astype(bf)
-    rx[0] = go(xs.at[0], xr.at[0], 0, rxr.at[0], x_dev)
     rf[1].wait_recv()
     total = delta(own[0]) + fr[1].astype(f32)
     for k in ORDER:
@@ -232,7 +239,8 @@
     px = over(pg, 3, pxr, None, (0,))
     py = first(pg, 2, pyr)
     my = first(mg, 4, myr)
-    mx = over(mg, 5, mxr, my, (0,))
+    arrived(mx[0])
+    mn = pass_on(mg, 4, mnr)
 
     pltpu.make_async_copy(arxy, arxy, asr.at[1]).wait()
     sq = sq + jnp.sum(arxy[...], axis=0)
@@ -247,7 +255,16 @@
         for c in range(2):
             share(zt, c)
 
-    to_planes(lambda zt: zt < z, share_both)
+    def share_below(lo, hi):
+        for zt in range(lo, hi):
+            pl.when(zt < z)(functools.partial(share_both, zt))
+
+    share_below(0, FIRST)
+    arrived(px[0])
+    pn = pass_on(pg, 2, pnr)
+    second(pg, 2, pyr, py)
+    px.update(over(pg, 3, pxr, py, (2, 6)))
+    share_below(FIRST, NZ)
     share(z, 1 - core)
 
     @pl.when(z < NZ - 1)
@@ -256,16 +273,11 @@
 
     to_planes(lambda zt: zt > z, share_both)
 
-    arrived(px[0])
-    q = pg.at[oth[0]]
-    pn = [go(q, q, 2, pnr.at[i], y_dev(k)) for i, k in enumerate((1, 7))]
-    second(pg, 2, pyr, py)
-    px.update(over(pg, 3, pxr, py, (2, 6)))
     second(mg, 4, myr, my)
-    mx.update(over(mg, 5, mxr, my, (2, 6, 1, 7)))
+    mx.update(over(mg, 5, mxr, my, (2, 6)))
     px.update(over(pg, 3, pxr, py, (3, 5, 4)))
     mx.update(over(mg, 5, mxr, my, (3, 5, 4)))
-    for cp in [py[1], py[7]] + pn + list(px.values()) + list(mx.values()):
+    for cp in [py[1], py[7], my[1], my[7]] + pn + mn + list(px.values()) + list(mx.values()):
         arrived(cp)
     for flow in range(7):
         drain(flow)
@@ -315,7 +327,7 @@
     dma = pltpu.SemaphoreType.DMA
     gathered = jax.ShapeDtypeStruct((REPS, BLK, HALF), bf)
     in_hbm = [pltpu.with_memory_space_constraint(v, pltpu.HBM) for v in (local, global_params, momentum)]
-    pg, mg, pown, factor = pl.pallas_call(
+    pg, mg, pown, factor, lv, gv, mv = pl.pallas_call(
         exchange,
         name="exchange",
         out_shape=[
@@ -323,15 +335,13 @@
             gathered,
             jax.ShapeDtypeStruct((BLK, HALF), f32),
             jax.ShapeDtypeStruct((8, 128), f32),
+            jax.ShapeDtypeStruct((ROWS, COLS), f32),
+            jax.ShapeDtypeStruct((ROWS, COLS), f32),
+            jax.ShapeDtypeStruct((SHARE, COLS), f32),
         ],
         in_specs=[hbm] * 3,
-        out_specs=[vmem] * 4,
-        scratch_shapes=[
-            pltpu.VMEM((ROWS, COLS), f32),
-            pltpu.VMEM((ROWS, COLS), f32),
-            pltpu.VMEM((SHARE, COLS), f32),
-        ]
-        + [pltpu.VMEM((NY, BLK, HALF), bf)] * 4
+        out_specs=[vmem] * 7,
+        scratch_shapes=[pltpu.VMEM((NY, BLK, HALF), bf)] * 4
         + [pltpu.VMEM((2, BLK, HALF), bf)] * 2
         + [
             pltpu.VMEM((2, 1, 128), f32),
@@ -347,6 +357,7 @@
             dma((2,)),
             dma((NY,)),
             dma((NY,)),
+            dma((2,)),
             dma((4,)),
             pltpu.SemaphoreType.REGULAR,
             pltpu.SemaphoreType.REGULAR((2, 2)),
@@ -377,7 +388,7 @@
             dma((2 * STEPS + 1,)),
         ],
         compiler_params=pltpu.CompilerParams(vmem_limit_bytes=16 << 20),
-    )(factor, pown, momentum, pg, mg, local, global_params)
+    )(factor, pown, mv, pg, mg, lv, gv)
     return (new_global, new_momentum, mixed[None])
 
 

time: 46.2 us -> 45.9 us (level)
  no operation moved by 1% of the time
where the time goes in v4:
time: 45.9 us; the launch traced here: 45.8 us
  Pallas kernels  45.1 us (98%)
  between operations  0.64 us (1%)
    pallas_call x1, Pallas kernels, shards(): pl.pallas_call(exchange, name='exchange', out_shape=[gathered, gathered,...  43.2 us
    pallas_call x1, Pallas kernels, shards(): pl.pallas_call(finish, name='finish', out_shape=[jax.ShapeDtypeStruct((RO...  1.9 us

profile of v4, /device:TPU:1, one launch (start us, length us, event | category | flops | bytes accessed | tf_op | source)
XLA Modules:
  0.0 45.8 jit_solution(7136414078048902510)
XLA Ops:
  0.6 43.2 %exchange.1 = (bf16[16,48,512]{2,1,0:T(8,128)(2,1)S(1)}, bf16[16,48,512]{2,1,0:T(8,128)(2,1)S(1)}, f32[48,512]{1,0:T(8,128)S(1)}, f32[8,128]{1,0:T(8,128)S(1)}, ...) custom-call(f32[384,1024]{1,0:T(8,128)} %bitcast.2, f32[384,1024]{1,0:T(8,128)} %global_hbm.1, ...), custom_call_target="tpu_custom_call" | custom-call | tf_op jit(solution)/shard_map/exchange/pallas_call | solution.py:330
  43.9 1.9 %finish.1 = (f32[384,1024]{1,0:T(8,128)}, f32[24,1024]{1,0:T(8,128)}, f32[384,1024]{1,0:T(8,128)}) custom-call(f32[8,128]{1,0:T(8,128)S(1)} %get-tuple-element.13.f_ref, f32[48,512]{1,0:T(8,128)S(1)} %get-tuple-element.14.pown, f32[24,1024]{1,0:T(8,128)S(1)} %get-tuple-element.15.mom, bf16[16,48,512]{2,1,0:T(8,128)(2,1)S(1)} %get-tuple-element.16.pg, ...), custom_call_target="tpu_custom_call" | custom-call | tf_op jit(solution)/shard_map/finish/pallas_call | solution.py:374

commit v5 on v4

--- a/solution.py
+++ b/solution.py
@@ -124,10 +124,10 @@
 
     sent = {}
 
-    def go(s, d, flow, rs, dev):
+    def go(s, d, flow, rs, dev, blocks=1):
         cp = remote(s, d, ssem.at[flow], rs, dev)
         cp.start()
-        sent[flow] = sent.get(flow, 0) + 1
+        sent[flow] = sent.get(flow, 0) + blocks
         return cp
 
     def drain(flow):
@@ -183,7 +183,21 @@
 
     hop_out(0)
     rf = [send_far(0)]
-    rx = {k: go(xs.at[k], xr.at[k], 0, rxr.at[k], x_dev) for k in ORDER}
+    def pieces(k):
+        if k not in ORDER[-2:]:
+            return [(0, HALF, k, 1)]
+        at = NY + 2 * ORDER[-2:].index(k)
+        return [(0, HALF // 2, at, 1), (HALF // 2, HALF, at + 1, 0)]
+
+    def send_piece(src_buf, dst_buf, k, piece, flow, sems, dev):
+        lo, hi, i, n = piece
+        cols = pl.ds(lo, hi - lo)
+        return go(src_buf.at[k, :, cols], dst_buf.at[k, :, cols], flow, sems.at[i], dev, n)
+
+    rx = {}
+    for k in ORDER:
+        for piece in pieces(k):
+            rx[k, piece[2]] = send_piece(xs, xr, k, piece, 0, rxr, x_dev)
     loads[2].wait()
     loads[3].wait()
     fs[1] = delta(own[FAR]).astype(bf)
@@ -207,9 +221,12 @@
             rf[0].wait_recv()
             xs[0] = (delta(oth[0]) + fr[0].astype(f32)).astype(bf)
             rx[0] = go(xs.at[0], xr.at[0], 0, rxr.at[0], x_dev)
-        rx[k].wait_recv()
-        ys[k] = (delta(own[k]) + xr[k].astype(f32)).astype(bf)
-        ry[k] = go(ys.at[k], yr.at[k], 1, ryr.at[k], y_dev(k))
+        mine_k = delta(own[k])
+        for piece in pieces(k):
+            lo, hi, i, _ = piece
+            rx[k, i].wait_recv()
+            ys[k, :, lo:hi] = (mine_k[:, lo:hi] + xr[k, :, lo:hi].astype(f32)).astype(bf)
+            ry[k, i] = send_piece(ys, yr, k, piece, 1, ryr, y_dev(k))
         if k == ORDER[2]:
             pl.semaphore_wait(pair, 1)
 
@@ -221,7 +238,8 @@
     rf[1].wait_recv()
     total = delta(own[0]) + fr[1].astype(f32)
     for k in ORDER:
-        ry[k].wait_recv()
+        for piece in pieces(k):
+            ry[k, piece[2]].wait_recv()
         total = total + yr[k].astype(f32)
     rx[0].wait_recv()
     total = total + xr[0].astype(f32)
@@ -349,8 +367,8 @@
             pltpu.VMEM((N_ZC + 1, 1, 128), f32),
             dma((5,)),
             dma((7,)),
-            dma((NY,)),
-            dma((NY,)),
+            dma((NY + 4,)),
+            dma((NY + 4,)),
             dma((2,)),
             dma((NY,)),
             dma((NY,)),

time: 45.9 us -> 46 us (level)
  no operation moved by 1% of the time
where the time goes in v5:
time: 46 us; the launch traced here: 45.9 us
  Pallas kernels  45.2 us (98%)
  between operations  0.64 us (1%)
    pallas_call x1, Pallas kernels, shards(): pl.pallas_call(exchange, name='exchange', out_shape=[gathered, gathered,...  43.3 us
    pallas_call x1, Pallas kernels, shards(): pl.pallas_call(finish, name='finish', out_shape=[jax.ShapeDtypeStruct((RO...  1.9 us

profile of v5, /device:TPU:1, one launch (start us, length us, event | category | flops | bytes accessed | tf_op | source)
XLA Modules:
  0.0 45.9 jit_solution(1723137657847230391)
XLA Ops:
  0.6 43.3 %exchange.1 = (bf16[16,48,512]{2,1,0:T(8,128)(2,1)S(1)}, bf16[16,48,512]{2,1,0:T(8,128)(2,1)S(1)}, f32[48,512]{1,0:T(8,128)S(1)}, f32[8,128]{1,0:T(8,128)S(1)}, ...) custom-call(f32[384,1024]{1,0:T(8,128)} %bitcast.2, f32[384,1024]{1,0:T(8,128)} %global_hbm.1, ...), custom_call_target="tpu_custom_call" | custom-call | tf_op jit(solution)/shard_map/exchange/pallas_call | solution.py:348
  44.0 1.9 %finish.1 = (f32[384,1024]{1,0:T(8,128)}, f32[24,1024]{1,0:T(8,128)}, f32[384,1024]{1,0:T(8,128)}) custom-call(f32[8,128]{1,0:T(8,128)S(1)} %get-tuple-element.13.f_ref, f32[48,512]{1,0:T(8,128)S(1)} %get-tuple-element.14.pown, f32[24,1024]{1,0:T(8,128)S(1)} %get-tuple-element.15.mom, bf16[16,48,512]{2,1,0:T(8,128)(2,1)S(1)} %get-tuple-element.16.pg, ...), custom_call_target="tpu_custom_call" | custom-call | tf_op jit(solution)/shard_map/finish/pallas_call | solution.py:392
